TPU v7x, 512 devices: a whole 4x4x16 slice. The times are simulated.
512 devices in a mesh: tm: 64 (over z, y_lo, core), sta: 8 (over x, y_hi).
Axes of the slice: x: 4, y: 4 (y_hi: 2, y_lo: 2; y = y_hi * 2 + y_lo), z: 16, core: 2. Of those that a mesh axis runs over, the one named last changes fastest.
Arguments:
- traces: float32 [48, 32768], P('sta', 'tm'), may hold values from -200 to 200
- bandpass_taps: float32 [128], replicated, may hold values from -0.5 to 0.5
- templates: bfloat16 [256, 48, 400], P(None, 'sta'), may hold values from -6 to 6
- moveouts: int32 [256, 48], P(None, 'sta'), may hold values from 0 to 400, as said below
- station_mask: int32 [16], P('sta'), may hold values 0 or 1
Outputs:
- network_stack: float32 [256, 32768], P('sta', 'tm')
Inputs may be any that keep to these rules, and one draw needn't show every extreme that they name: `moveouts`: every template has offset 0 on some channel and 400 on another.
All inputs are finite; a program needn't handle non-finite values. No bound on the sum of `station_mask` on one device may be relied on, other than what follows from the above.
Results may differ from a plain program's by a relative error of at most 0.0041.
Values sent between devices are 32-bit elements; how exact they have to be, the bound alone decides.
A program may use at most 64 MiB of HBM per device.

v0:
```python
import math

import jax
import jax.numpy as jnp
from jax import lax
from jax.sharding import PartitionSpec as P

TLEN = 400
DMAX = 400


def passed_along(x, axis, by):
    length = lax.axis_size(axis)
    pairs = [(i, i + by) for i in range(length) if 0 <= i + by < length]
    return lax.ppermute(x, axis, pairs)


def sliding_windows(signals, length, columns):
    channel_count, extent = signals.shape
    repeated = jnp.broadcast_to(signals[:, None, :], (channel_count, length, extent))
    flattened = jnp.pad(repeated.reshape(channel_count, length * extent), ((0, 0), (0, length)))
    return flattened.reshape(channel_count, length, extent + 1)[:, :, :columns]


def bandpass_local(samples, reversed_taps, columns):
    windows = sliding_windows(samples, reversed_taps.shape[0], columns)
    return jnp.einsum("i,ciu->cu", reversed_taps, windows, precision=lax.Precision.HIGHEST)


def unit_templates(templates):
    values = templates.astype(jnp.float32)
    centred = values - jnp.mean(values, axis=-1, keepdims=True)
    factor = lax.rsqrt(jnp.mean(centred * centred, axis=-1, keepdims=True) + 1e-06) * (
        1.0 / math.sqrt(TLEN)
    )
    return (centred * factor).astype(jnp.bfloat16)


def shift_rows_left(values, delays, largest):
    extent = values.shape[-1]
    result = values
    for bit_number in range(max(largest, 1).bit_length()):
        step_len = 1 << bit_number
        moved = jnp.concatenate(
            [result[..., step_len:], jnp.zeros(result.shape[:-1] + (step_len,), result.dtype)],
            axis=-1,
        )
        taken = (delays // step_len % 2 == 1)[..., None]
        result = jnp.where(taken, moved, result)
    return result


def per_device(traces, bandpass_taps, templates, moveouts, station_mask):
    channel_count, slab_len = traces.shape
    tap_count = bandpass_taps.shape[0]
    reversed_taps = bandpass_taps[::-1]
    rim_len = TLEN - 1
    past_rim = passed_along(traces[:, slab_len - (tap_count - 1) :], "tm", 1)
    filtered = bandpass_local(jnp.concatenate([past_rim, traces], axis=1), reversed_taps, slab_len)
    ahead_rim = passed_along(filtered[:, :rim_len], "tm", -1)
    series = jnp.concatenate([filtered, ahead_rim], axis=1)
    unit = unit_templates(templates)
    template_count = templates.shape[0]
    station_count = station_mask.shape[0]

    def add_station(station, partials):
        own_part, spill_part = partials
        station_rows = lax.dynamic_slice_in_dim(series, 3 * station, 3, 0)
        windows = sliding_windows(station_rows, TLEN, slab_len)
        window_sum = jnp.sum(windows, axis=1)
        window_power = jnp.sum(windows * windows, axis=1)
        inverse_norm = lax.rsqrt(jnp.maximum(window_power - window_sum * window_sum / TLEN, 1.0))
        kernels = lax.dynamic_slice_in_dim(unit, 3 * station, 3, 1)
        products = jnp.einsum(
            "kcj,cju->kcu",
            kernels,
            windows.astype(jnp.bfloat16),
            preferred_element_type=jnp.float32,
        )
        correlation = products * inverse_norm[None]
        padded_corr = jnp.concatenate(
            [jnp.zeros((template_count, 3, DMAX), jnp.float32), correlation], axis=2
        )
        delays = lax.dynamic_slice_in_dim(moveouts, 3 * station, 3, 1)
        moved = shift_rows_left(padded_corr, delays, DMAX)
        available = lax.dynamic_index_in_dim(station_mask, station, 0, keepdims=False).astype(
            jnp.float32
        )
        combined = jnp.sum(moved, axis=1) * available
        return (own_part + combined[:, DMAX:], spill_part + combined[:, :DMAX])

    zeros_own = jnp.zeros((template_count, slab_len), jnp.float32)
    zeros_spill = jnp.zeros((template_count, DMAX), jnp.float32)
    own_part, spill_part = lax.fori_loop(0, station_count, add_station, (zeros_own, zeros_spill))
    from_right = passed_along(spill_part, "tm", -1)
    joined = jnp.concatenate(
        [own_part[:, : slab_len - DMAX], own_part[:, slab_len - DMAX :] + from_right], axis=1
    )
    return lax.psum_scatter(joined, "sta", scatter_dimension=0, tiled=True)


def solution(mesh):
    in_specs = (P("sta", "tm"), P(), P(None, "sta", None), P(None, "sta"), P("sta"))
    out_specs = P("sta", "tm")
    return jax.shard_map(
        per_device, mesh=mesh, in_specs=in_specs, out_specs=out_specs, check_vma=False
    )
```

profile of v0, /device:TPU:2, one launch (start us, length us, event | category | flops | bytes accessed | tf_op | source)
XLA Modules:
  0.0 223.1 jit_solution(5461943383163435440)
XLA Ops:
  6.5 0.8 slice.147
  7.3 1.7 collective-permute-start
  9.0 1.5 convert_reduce_fusion
  10.5 1.6 fusion.29
  12.1 0.7 rev.3
  12.9 0.8 pad_maximum_fusion.2
  13.7 1.4 broadcast_in_dim.222
  15.1 3.0 %reshape.69 = f32[6,81792]{1,0:T(8,128)S(1)} reshape(f32[6,128,639]{2,1,0:T(8,128)} %broadcast_in_dim.222) | data formatting | bytes 3926016 | tf_op jit(solution)/shard_map/reshape | solution.py:21
  18.3 0.4 copy.13
  18.7 0.9 fusion.31
  19.6 1.3 collective-permute-start.1
  20.9 0.3 fusion.30
  21.3 2.8 %collective-permute-done.1 = f32[6,399]{1,0:T(8,128)S(1)} collective-permute-done((f32[6,399]{1,0:T(8,128)S(1)}, f32[6,399]{1,0:T(8,128)S(1)}, u32[]{:S(2)}, u32[]{:S(2)}) %collective-permute-start.1) | collective-permute-done | bytes 9608 | tf_op jit(solution)/shard_map/ppermute | solution.py:15
  24.1 84.5 %while.19 = (s32[]{:T(128)}, f32[256,512]{0,1:T(8,128)S(1)}, f32[256,400]{0,1:T(8,128)S(1)}, s32[256,6]{0,1:T(8,128)S(1)}, f32[6,911]{1,0:T(8,128)S(1)}, /*index...) while((s32[]{:T(128)}, f32[256,512]{0,1:T(8,128)S(1)}, ...), condition=%wide.region_6.7_spmd.clone, body=%wide.region_2.6_spmd.clone.sunk | while | flops 324427776 | bytes 158305280 | solution.py:94
  24.3 2.8 %broadcast_in_dim.261 = f32[3,400,911]{2,1,0:T(8,128)} broadcast(f32[3,911]{1,0:T(4,128)S(1)} %constant_dynamic-slice_fusion.2), dimensions={0,2} | broadcast | bytes 4383732 | tf_op jit(solution)/shard_map/while/body/eval_jaxpr/broadcast_in_dim | solution.py:20
  27.1 10.4 %reshape.77 = f32[3,364400]{1,0:T(4,128)} reshape(f32[3,400,911]{2,1,0:T(8,128)} %broadcast_in_dim.261) | data formatting | bytes 8745600 | tf_op jit(solution)/shard_map/while/body/eval_jaxpr/reshape | solution.py:21
  37.5 7.1 %pad.101 = f32[3,364800]{1,0:T(4,128)} pad(f32[3,364400]{1,0:T(4,128)} %reshape.77, f32[]{:T(128)} %constant.452.clone.1..sunk), padding=0_0x0_400 | pad | bytes 8750404 | tf_op jit(solution)/shard_map/while/body/eval_jaxpr/jit(_pad)/pad | solution.py:21
  44.6 10.5 %reshape.78 = f32[3,400,912]{2,1,0:T(8,128)} reshape(f32[3,364800]{1,0:T(4,128)} %pad.101) | data formatting | bytes 8755200 | tf_op jit(solution)/shard_map/while/body/eval_jaxpr/reshape | solution.py:22
  55.1 2.0 slice_reduce_fusion.2
  57.1 2.5 %multiply_bitcast_fusion.2 = f32[256,3,512]{0,2,1:T(8,128)S(1)} fusion(f32[3,400,912]{2,1,0:T(8,128)} %reshape.78, f32[3,512]{1,0:T(4,128)S(1)} %maximum_rsqrt_fusion.2, bf16[256,6,400]{0,2,1:T(8,128)(2,1)S(1)} %get-tuple-element.385, s32[]{:T(128)S(6)} %select_n.468), kind=kOutput, calls=%fused_computation.13.clone.1 | convolution fusion | flops 314966016 | bytes 3424260 | tf_op jit(solution)/shard_map/while/body/eval_jaxpr/kcj,cju->kcu/dot_general | solution.py:74
  59.6 0.2 pad_slice_fusion.2
  59.9 0.3 pad_select_fusion.16
  60.3 0.2 slice.207
  60.5 0.4 pad_select_fusion.17
  60.8 0.2 slice.208
  61.1 0.4 pad_select_fusion.18
  61.5 0.2 slice.209
  61.7 0.4 pad_select_fusion.19
  62.1 0.2 slice.210
  62.3 0.4 pad_select_fusion.20
  62.6 0.2 slice.211
  62.8 0.4 pad_select_fusion.21
  63.4 0.4 pad_select_fusion.22
  63.9 0.3 pad_select_fusion.23
  64.4 0.3 select_reduce_fusion.2
  64.7 0.7 dynamic_slice.82
  66.5 2.8 %broadcast_in_dim.261 = f32[3,400,911]{2,1,0:T(8,128)} broadcast(f32[3,911]{1,0:T(4,128)S(1)} %constant_dynamic-slice_fusion.2), dimensions={0,2} | broadcast | bytes 4383732 | tf_op jit(solution)/shard_map/while/body/eval_jaxpr/broadcast_in_dim | solution.py:20
  69.3 10.4 %reshape.77 = f32[3,364400]{1,0:T(4,128)} reshape(f32[3,400,911]{2,1,0:T(8,128)} %broadcast_in_dim.261) | data formatting | bytes 8745600 | tf_op jit(solution)/shard_map/while/body/eval_jaxpr/reshape | solution.py:21
  79.7 7.1 %pad.101 = f32[3,364800]{1,0:T(4,128)} pad(f32[3,364400]{1,0:T(4,128)} %reshape.77, f32[]{:T(128)} %constant.452.clone.1..sunk), padding=0_0x0_400 | pad | bytes 8750404 | tf_op jit(solution)/shard_map/while/body/eval_jaxpr/jit(_pad)/pad | solution.py:21
  86.7 10.5 %reshape.78 = f32[3,400,912]{2,1,0:T(8,128)} reshape(f32[3,364800]{1,0:T(4,128)} %pad.101) | data formatting | bytes 8755200 | tf_op jit(solution)/shard_map/while/body/eval_jaxpr/reshape | solution.py:22
  97.2 2.0 slice_reduce_fusion.2
  99.3 2.5 %multiply_bitcast_fusion.2 = f32[256,3,512]{0,2,1:T(8,128)S(1)} fusion(f32[3,400,912]{2,1,0:T(8,128)} %reshape.78, f32[3,512]{1,0:T(4,128)S(1)} %maximum_rsqrt_fusion.2, bf16[256,6,400]{0,2,1:T(8,128)(2,1)S(1)} %get-tuple-element.385, s32[]{:T(128)S(6)} %select_n.468), kind=kOutput, calls=%fused_computation.13.clone.1 | convolution fusion | flops 314966016 | bytes 3424260 | tf_op jit(solution)/shard_map/while/body/eval_jaxpr/kcj,cju->kcu/dot_general | solution.py:74
  101.8 0.2 pad_slice_fusion.2
  102.1 0.3 pad_select_fusion.16
  102.4 0.2 slice.207
  102.7 0.4 pad_select_fusion.17
  103.0 0.2 slice.208
  103.3 0.4 pad_select_fusion.18
  103.6 0.2 slice.209
  103.9 0.4 pad_select_fusion.19
  104.2 0.2 slice.210
  104.5 0.4 pad_select_fusion.20
  105.0 0.4 pad_select_fusion.21
  105.6 0.4 pad_select_fusion.22
  106.1 0.3 pad_select_fusion.23
  106.6 0.3 select_reduce_fusion.2
  106.9 0.7 dynamic_slice.82
  108.6 0.2 copy.8
  108.8 1.3 collective-permute-start.2
  110.1 0.2 copy.6
  110.4 4.3 %collective-permute-done.2 = f32[256,400]{1,0:T(8,128)S(1)} collective-permute-done((f32[256,400]{1,0:T(8,128)S(1)}, f32[256,400]{1,0:T(8,128)S(1)}, u32[]{:S(2)}, u32[]{:S(2)}) %collective-permute-start.2) | collective-permute-done | bytes 409632 | tf_op jit(solution)/shard_map/ppermute | solution.py:15
  114.6 0.2 slice_add_fusion.2
  114.8 1.0 pad_maximum_fusion
  115.8 100.4 %reduce-scatter.2.cloned.1.call-done = f32[32,512]{1,0:T(8,128)} async-done(((f32[256,512]{1,0:T(8,128)}), f32[32,512]{1,0:T(8,128)}) %reduce-scatter.2.cloned.1.call-update) | async-done | bytes 65552 | tf_op jit(solution)/shard_map/reduce_scatter | solution.py:99
  (38 shorter events, 2.2 us)
Async XLA Ops:
  6.5 209.8 %reduce-scatter.2.cloned.1.call-start = ((), (), s32[]{:S(2)}) async-start(), calls=%async_computation.1 | async-start | bytes 589824 | tf_op jit(solution)/shard_map/reduce_scatter | solution.py:99
  7.3 5.6 %collective-permute-start = (f32[6,127]{1,0:T(8,128)S(1)}, f32[6,127]{1,0:T(8,128)S(1)}, u32[]{:S(2)}, u32[]{:S(2)}) collective-permute-start(f32[6,127]{1,0:T(8,128)S(1)} %slice.147), channel_id=1, source_target_pairs={{0,8},{8,16},{16,24},{24,32},{32,40},{40,48},{48,56},{56,64},{64,7... | collective-permute-start | bytes 9152 | tf_op jit(solution)/shard_map/ppermute | solution.py:15
  18.3 2.7 %copy-start = (bf16[256,6,400]{0,2,1:T(8,128)(2,1)S(1)}, bf16[256,6,400]{0,2,1:T(8,128)(2,1)}, u32[]{:S(2)}) copy-start(bf16[256,6,400]{0,2,1:T(8,128)(2,1)} %param.9) | copy-start | bytes 3686404
  18.7 5.4 %copy-start.1 = (s32[256,6]{0,1:T(8,128)S(1)}, s32[256,6]{0,1:T(8,128)}, u32[]{:S(2)}) copy-start(s32[256,6]{0,1:T(8,128)} %param.10) | copy-start | bytes 18436
  18.7 5.4 %copy-start.2 = (s32[2]{0:T(128)S(1)}, s32[2]{0:T(128)}, u32[]{:S(2)}) copy-start(s32[2]{0:T(128)} %param.11) | copy-start | bytes 28
  19.6 4.4 %collective-permute-start.1 = (f32[6,399]{1,0:T(8,128)S(1)}, f32[6,399]{1,0:T(8,128)S(1)}, u32[]{:S(2)}, u32[]{:S(2)}) collective-permute-start(f32[6,399]{1,0:T(8,128)S(1)} %bitcast.20), channel_id=1, source_target_pairs={{8,0},{16,8},{24,16},{32,24},{40,32},{48,40},{56,48},{64,56},{72,6... | collective-permute-start | bytes 28736 | tf_op jit(solution)/shard_map/ppermute | solution.py:15
  108.8 5.8 %collective-permute-start.2 = (f32[256,400]{1,0:T(8,128)S(1)}, f32[256,400]{1,0:T(8,128)S(1)}, u32[]{:S(2)}, u32[]{:S(2)}) collective-permute-start(f32[256,400]{1,0:T(8,128)S(1)} %copy.8), channel_id=1, source_target_pairs={{8,0},{16,8},{24,16},{32,24},{40,32},{48,40},{56,48},{64,56},{72,6... | collective-permute-start | bytes 1228808 | tf_op jit(solution)/shard_map/ppermute | solution.py:15
Sparse Core Ops, SparseCore 0:
  116.0 100.2 reduce-scatter.1
where the time goes:
time: 224 us; the launch traced here: 223 us
  waiting for transfers between devices  107 us (48%)
  local copies, waits for them, and re-layouts  73.3 us (33%)
  other arithmetic  16.6 us (7%)
  between operations  13.6 us (6%)
  matrix products  5.89 us (3%)
  starting transfers between devices  4.31 us (2%)
    reduce_scatter x1, waiting for transfers between devices, per_device(): return lax.psum_scatter(joined, 'sta', scatter_dimension=0, tiled=True)  100 us
    reshape x3, local copies, waits for them, and re-layouts, sliding_windows(): repeated.reshape(channel_count, length * extent)  23.8 us
    reshape x2, local copies, waits for them, and re-layouts, sliding_windows(): return flattened.reshape(channel_count, length, extent + 1)[:, :, :columns]  21 us
    pad x3, local copies, waits for them, and re-layouts, sliding_windows(): jnp.pad(repeated.reshape(channel_count, length * extent), ((0, 0), (0, le...  14.3 us
    broadcast_in_dim x3, local copies, waits for them, and re-layouts, sliding_windows(): jnp.broadcast_to(signals[:, None, :], (channel_count, length, extent))  7.04 us
    ppermute x3, waiting for transfers between devices, passed_along(): return lax.ppermute(x, axis, pairs)  7.02 us
    select_n x16, other arithmetic, shift_rows_left(): result = jnp.where(taken, moved, result)  5.57 us
    dot_general x2, matrix products, add_station(): jnp.einsum('kcj,cju->kcu', kernels, windows.astype(jnp.bfloat16), preferr...  4.96 us
  transfers between devices with their start and end apart: 4, of which 3 were waited for; matrix products, arithmetic and copies ran while one was open for 2% of the time, Pallas kernels for 0%

commit v1 on v0

v1 whole, which is shorter than its diff:
```python
import functools
import math

import jax
import jax.numpy as jnp
from jax import lax
from jax.experimental import pallas as pl
from jax.experimental.pallas import tpu as pltpu
from jax.sharding import PartitionSpec as P

TLEN = 400
DMAX = 400
LANE = 128
MESH = pl.DeviceIdType.MESH


def shifted_left(values, step):
    extent = values.shape[-1]
    if step % LANE == 0:
        return jnp.concatenate([values[:, step:], values[:, :step]], axis=1)
    return pltpu.roll(values, extent - step, 1)


def toeplitz(taps):
    rows = jnp.broadcast_to(taps, (LANE, LANE))
    turned = pltpu.roll(rows, 0, 1, stride=1, stride_axis=0)
    row = lax.broadcasted_iota(jnp.int32, (LANE, LANE), 0)
    lane = lax.broadcasted_iota(jnp.int32, (LANE, LANE), 1)
    below = jnp.where(lane >= row, turned, 0.0)
    above = jnp.where(lane < row, turned, 0.0)
    return jnp.concatenate([above, below], axis=0)


def kernel(
    sizes,
    traces_ref,
    taps_ref,
    templates_ref,
    moveouts_ref,
    mask_ref,
    out_ref,
    window,
    raw_templates,
    unit,
    hankel,
    partial,
    received,
    template_sem,
    halo_send,
    halo_recv,
    sum_send,
    sum_recv,
):
    tm_count, sta_count, slab, channels, share = sizes
    x_count = sta_count // 2
    kcount = share * sta_count
    me_t = lax.axis_index("tm")
    me_s = lax.axis_index("sta")
    my_x, my_y = me_s // 2, lax.rem(me_s, 2)

    def time_device(by):
        return lax.rem(me_t + by + tm_count, tm_count)

    def station_device(dx, dy):
        return 2 * lax.rem(my_x + dx, x_count) + lax.rem(my_y + dy, 2)

    offsets = [(dx, dy) for dx in range(x_count) for dy in range(2) if (dx, dy) != (0, 0)]

    barrier = pltpu.get_barrier_semaphore()
    for by in (-2, -1, 1, 2):
        pl.semaphore_signal(
            barrier, inc=1, device_id={"tm": time_device(by)}, device_id_type=MESH
        )
    for dx, dy in offsets:
        pl.semaphore_signal(
            barrier, inc=1, device_id={"sta": station_device(dx, dy)}, device_id_type=MESH
        )
    fetch = pltpu.make_async_copy(templates_ref, raw_templates, template_sem)
    fetch.start()

    window[0:channels, LANE : LANE + slab] = traces_ref[...]
    window[channels:8, LANE : LANE + slab] = jnp.zeros((8 - channels, slab), jnp.float32)
    bands = toeplitz(taps_ref[...])
    pl.semaphore_wait(barrier, 4 + len(offsets))

    def halo(slot, by, src, dst, width):
        return pltpu.make_async_remote_copy(
            src_ref=window.at[:, pl.ds(src, width)],
            dst_ref=window.at[:, pl.ds(dst, width)],
            send_sem=halo_send.at[slot],
            recv_sem=halo_recv.at[slot],
            device_id={"tm": time_device(by)},
            device_id_type=MESH,
        )

    rest = 11 * LANE + LANE - (LANE + 2 * slab)
    halos = [
        halo(0, -2, LANE, LANE + 2 * slab, rest),
        halo(1, -1, LANE, LANE + slab, slab),
        halo(2, 1, slab, 0, LANE),
    ]
    for copy in halos:
        copy.start()

    fetch.wait()
    for c in range(channels):
        values = raw_templates[c].astype(jnp.float32)
        mean = jnp.sum(values, axis=0, keepdims=True) * (1.0 / TLEN)
        centred = values - mean
        power = jnp.sum(centred * centred, axis=0, keepdims=True) * (1.0 / TLEN)
        factor = lax.rsqrt(power + 1e-06) * (1.0 / math.sqrt(TLEN))
        scaled = centred * factor
        padded = jnp.concatenate(
            [scaled, jnp.zeros((512 - TLEN, kcount), jnp.float32)], axis=0
        )
        unit[c] = jnp.transpose(padded).astype(jnp.bfloat16)
    delays = jnp.transpose(
        jnp.concatenate(
            [moveouts_ref[...], jnp.zeros((8 - channels, kcount), jnp.int32)], axis=0
        )
    )

    for copy in halos:
        copy.wait()

    first = jnp.where(me_t == 0, 0.0, window[:, 0:LANE])
    raw = [first] + [window[:, LANE * b : LANE * (b + 1)] for b in range(1, 12)]
    lows = jnp.concatenate(raw[:11], axis=0)
    highs = jnp.concatenate(raw[1:], axis=0)
    filtered = jnp.dot(
        jnp.concatenate([lows, highs], axis=1),
        bands,
        precision=lax.Precision.HIGHEST,
        preferred_element_type=jnp.float32,
    )
    remaining = (tm_count - me_t) * slab
    blocks = [
        jnp.where(b * LANE < remaining, filtered[8 * b : 8 * b + 8], 0.0) for b in range(11)
    ]
    series = jnp.concatenate(blocks, axis=1)

    level = jnp.concatenate([series, series * series], axis=0)
    kept = {}
    for bit in range(9):
        if bit in (4, 7, 8):
            kept[bit] = level
        if bit < 8:
            level = level + shifted_left(level, 1 << bit)
    sums = kept[8] + shifted_left(kept[7], 256) + shifted_left(kept[4], 384)
    window_sum, window_power = sums[0:8, : 8 * LANE], sums[8:16, : 8 * LANE]
    inverse_norm = lax.rsqrt(
        jnp.maximum(window_power - window_sum * window_sum * (1.0 / TLEN), 1.0)
    )
    row = lax.broadcasted_iota(jnp.int32, (8, 8 * LANE), 0)
    weight = jnp.where(row < 3, mask_ref[0], mask_ref[1]).astype(jnp.float32)
    inverse_norm = inverse_norm * weight

    lane = lax.broadcasted_iota(jnp.int32, (LANE, LANE), 1)
    line = lax.broadcasted_iota(jnp.int32, (LANE, LANE), 0)
    inside = lane + line < LANE
    turn = lax.rem(lane + line, LANE)
    for c in range(channels):
        turned = [
            jnp.take_along_axis(
                jnp.broadcast_to(blocks[b][c : c + 1], (LANE, LANE)),
                turn,
                axis=1,
                mode="promise_in_bounds",
            )
            for b in range(11)
        ]
        turned.append(jnp.zeros((LANE, LANE), jnp.float32))
        for b in range(11):
            hankel[c, :, LANE * b : LANE * (b + 1)] = jnp.where(
                inside, turned[b], turned[b + 1]
            ).astype(jnp.bfloat16)

    lane_k = lax.broadcasted_iota(jnp.int32, (kcount, LANE), 1)
    total = [jnp.zeros((kcount, LANE), jnp.float32) for _ in range(4)]
    for c in range(channels):
        matrix = jnp.concatenate(
            [hankel[c, :, LANE * m : LANE * (m + 8)] for m in range(4)], axis=0
        )
        products = jnp.dot(unit[c], matrix, preferred_element_type=jnp.float32)
        delay = jnp.broadcast_to(delays[:, c : c + 1], (kcount, LANE))
        by_256 = delay >= 256
        by_128 = lax.rem(delay, 256) >= 128
        fine = lax.rem(delay, 128)
        p = [
            products[:, LANE * b : LANE * (b + 1)] * inverse_norm[c : c + 1, LANE * b : LANE * (b + 1)]
            for b in range(8)
        ]
        p = [jnp.where(by_256, p[b + 2], p[b]) for b in range(6)]
        p = [jnp.where(by_128, p[b + 1], p[b]) for b in range(5)]
        source = lax.rem(lane_k + fine, LANE)
        ahead = lane_k < fine
        for b in range(4):
            joined = jnp.where(ahead, p[b + 1], p[b])
            total[b] = total[b] + jnp.take_along_axis(
                joined, source, axis=1, mode="promise_in_bounds"
            )
    for b in range(4):
        partial[:, LANE * b : LANE * (b + 1)] = total[b]

    copies = []
    for slot, (dx, dy) in enumerate(offsets):
        peer = station_device(dx, dy)
        copy = pltpu.make_async_remote_copy(
            src_ref=partial.at[pl.ds(pl.multiple_of(peer * share, share), share)],
            dst_ref=received.at[slot],
            send_sem=sum_send.at[slot],
            recv_sem=sum_recv.at[slot],
            device_id={"sta": peer},
            device_id_type=MESH,
        )
        copy.start()
        copies.append(copy)
    result = partial[pl.ds(pl.multiple_of(me_s * share, share), share), :]
    for slot, copy in enumerate(copies):
        copy.wait()
        result = result + received[slot]
    out_ref[...] = result


def per_device(sizes, traces, taps, templates, moveouts, mask):
    tm_count, sta_count, slab, channels, share = sizes
    kcount = share * sta_count
    vmem = pl.BlockSpec(memory_space=pltpu.VMEM)
    return pl.pallas_call(
        functools.partial(kernel, sizes),
        out_shape=jax.ShapeDtypeStruct((share, slab), jnp.float32),
        in_specs=[
            vmem,
            vmem,
            pl.BlockSpec(memory_space=pl.ANY),
            vmem,
            pl.BlockSpec(memory_space=pltpu.SMEM),
        ],
        out_specs=vmem,
        scratch_shapes=[
            pltpu.VMEM((8, 12 * LANE), jnp.float32),
            pltpu.VMEM((channels, TLEN, kcount), jnp.bfloat16),
            pltpu.VMEM((channels, kcount, 512), jnp.bfloat16),
            pltpu.VMEM((channels, LANE, 11 * LANE), jnp.bfloat16),
            pltpu.VMEM((kcount, slab), jnp.float32),
            pltpu.VMEM((sta_count - 1, share, slab), jnp.float32),
            pltpu.SemaphoreType.DMA,
            pltpu.SemaphoreType.DMA((3,)),
            pltpu.SemaphoreType.DMA((3,)),
            pltpu.SemaphoreType.DMA((sta_count - 1,)),
            pltpu.SemaphoreType.DMA((sta_count - 1,)),
        ],
        compiler_params=pltpu.CompilerParams(
            collective_id=0, has_side_effects=True, vmem_limit_bytes=48 * 2**20
        ),
        cost_estimate=pl.CostEstimate(
            flops=2 * kcount * channels * 512 * 1024, bytes_accessed=4 * 2**20, transcendentals=0
        ),
        name="network_match",
    )(
        traces,
        taps.reshape(1, LANE),
        jnp.transpose(templates, (1, 2, 0)),
        jnp.transpose(moveouts),
        mask,
    )


def solution(mesh):
    tm_count, sta_count = mesh.shape["tm"], mesh.shape["sta"]

    def run(traces, taps, templates, moveouts, mask):
        sizes = (
            tm_count,
            sta_count,
            traces.shape[1] // tm_count,
            traces.shape[0] // sta_count,
            templates.shape[0] // sta_count,
        )
        return jax.shard_map(
            functools.partial(per_device, sizes),
            mesh=mesh,
            in_specs=(P("sta", "tm"), P(), P(None, "sta", None), P(None, "sta"), P("sta")),
            out_specs=P("sta", "tm"),
            check_vma=False,
        )(traces, taps, templates, moveouts, mask)

    return run
```

time: 224 us -> 33.9 us (0.15)
  the two profiles are of different devices: /device:TPU:2 before, /device:TPU:4 now
where the time goes in v1:
time: 33.9 us; the launch traced here: 33.6 us
  Pallas kernels  29 us (86%)
  local copies, waits for them, and re-layouts  4.64 us (14%)
    pallas_call x1, Pallas kernels, per_device(): pl.pallas_call(functools.partial(kernel, sizes), out_shape=jax.ShapeDtype...  29 us
    unnamed x11, local copies, waits for them, and re-layouts  4.64 us

profile of v1, /device:TPU:4, one launch (start us, length us, event | category | flops | bytes accessed | tf_op | source)
XLA Modules:
  0.0 33.6 jit_solution(5078901524182356507)
XLA Ops:
  0.0 0.0 copy-start
  0.0 1.3 %copy-done = bf16[256,6,400]{0,2,1:T(8,128)(2,1)S(1)} copy-done((bf16[256,6,400]{0,2,1:T(8,128)(2,1)S(1)}, bf16[256,6,400]{0,2,1:T(8,128)(2,1)}, u32[]{:S(2)}) %copy-start) | copy-done | bytes 1228824
  1.3 0.0 copy-start.1
  1.3 0.7 %copy-done.1 = f32[6,512]{1,0:T(8,128)S(1)} copy-done((f32[6,512]{1,0:T(8,128)S(1)}, f32[6,512]{1,0:T(8,128)}, u32[]{:S(2)}) %copy-start.1) | copy-done | bytes 12312
  2.0 0.0 copy-start.2
  2.0 0.7 %copy-done.2 = s32[256,6]{0,1:T(8,128)S(1)} copy-done((s32[256,6]{0,1:T(8,128)S(1)}, s32[256,6]{0,1:T(8,128)}, u32[]{:S(2)}) %copy-start.2) | copy-done | bytes 6168
  2.7 0.0 copy-start.3
  2.7 0.7 %copy-done.3 = f32[128]{0:T(128)S(1)} copy-done((f32[128]{0:T(128)S(1)}, f32[128]{0:T(128)}, u32[]{:S(2)}) %copy-start.3) | copy-done | bytes 536
  3.4 0.0 copy-start.4
  3.4 0.7 %copy-done.4 = s32[2]{0:T(128)S(1)} copy-done((s32[2]{0:T(128)S(1)}, s32[2]{0:T(128)}, u32[]{:S(2)}) %copy-start.4) | copy-done | bytes 32
  4.0 29.0 %network_match.1 = f32[32,512]{1,0:T(8,128)S(1)} custom-call(f32[6,512]{1,0:T(8,128)S(1)} %copy-done.1, f32[1,128]{1,0:T(1,128)S(1)} %bitcast.5, bf16[6,400,256]{2,1,0:T(8,128)(2,1)S(1)} %bitcast.3, s32[6,256]{1,0:T(8,128)S(1)} %bitcast.4, s32[2]{0:T(128)S(1)} %copy-done.4), custom_call_target="tpu_custom_call" | custom-call | flops 1610612736 | bytes 4194304 | tf_op jit(solution)/shard_map/network_match/pallas_call | solution.py:229
  33.0 0.6 %copy.7 = f32[32,512]{1,0:T(8,128)} copy(f32[32,512]{1,0:T(8,128)S(1)} %network_match.1) | data formatting | bytes 131072
Async XLA Ops:
  0.0 1.3 %copy-start = (bf16[256,6,400]{0,2,1:T(8,128)(2,1)S(1)}, bf16[256,6,400]{0,2,1:T(8,128)(2,1)}, u32[]{:S(2)}) copy-start(bf16[256,6,400]{0,2,1:T(8,128)(2,1)} %param.7) | copy-start | bytes 3686404
  1.3 0.7 %copy-start.1 = (f32[6,512]{1,0:T(8,128)S(1)}, f32[6,512]{1,0:T(8,128)}, u32[]{:S(2)}) copy-start(f32[6,512]{1,0:T(8,128)} %traces_ref.1) | copy-start | bytes 36868
  2.0 0.7 %copy-start.2 = (s32[256,6]{0,1:T(8,128)S(1)}, s32[256,6]{0,1:T(8,128)}, u32[]{:S(2)}) copy-start(s32[256,6]{0,1:T(8,128)} %param.8) | copy-start | bytes 18436
  2.7 0.7 %copy-start.3 = (f32[128]{0:T(128)S(1)}, f32[128]{0:T(128)}, u32[]{:S(2)}) copy-start(f32[128]{0:T(128)} %param.6) | copy-start | bytes 1540
  3.4 0.7 %copy-start.4 = (s32[2]{0:T(128)S(1)}, s32[2]{0:T(128)}, u32[]{:S(2)}) copy-start(s32[2]{0:T(128)} %mask_ref.1) | copy-start | bytes 28

commit v2 on v1

v2 whole, which is shorter than its diff:
```python
import functools
import math

import jax
import jax.numpy as jnp
from jax import lax
from jax.experimental import pallas as pl
from jax.experimental.pallas import tpu as pltpu
from jax.sharding import PartitionSpec as P

TLEN = 400
DMAX = 400
LANE = 128
BLOCKS = 11
CHUNKS = (4, 4)
MESH = pl.DeviceIdType.MESH


def shifted_left(values, step):
    extent = values.shape[-1]
    if step % LANE == 0:
        return jnp.concatenate([values[:, step:], values[:, :step]], axis=1)
    return pltpu.roll(values, extent - step, 1)


def toeplitz(taps):
    rows = jnp.broadcast_to(taps, (LANE, LANE))
    turned = pltpu.roll(rows, 0, 1, stride=1, stride_axis=0)
    row = lax.broadcasted_iota(jnp.int32, (LANE, LANE), 0)
    lane = lax.broadcasted_iota(jnp.int32, (LANE, LANE), 1)
    below = jnp.where(lane >= row, turned, 0.0)
    above = jnp.where(lane < row, turned, 0.0)
    return jnp.concatenate([above, below], axis=0)


def position():
    return lax.axis_index("tm"), lax.axis_index("sta")


class Places:
    def __init__(self, sizes):
        self.tm_count, self.sta_count = sizes[0], sizes[1]
        self.x_count = self.sta_count // 2
        self.me_t, self.me_s = position()
        self.offsets = [
            (dx, dy) for dx in range(self.x_count) for dy in range(2) if (dx, dy) != (0, 0)
        ]

    def time_device(self, by):
        return lax.rem(self.me_t + by + self.tm_count, self.tm_count)

    def station_device(self, dx, dy):
        x = lax.rem(self.me_s // 2 + dx, self.x_count)
        return 2 * x + lax.rem(lax.rem(self.me_s, 2) + dy, 2)


def greet(places):
    barrier = pltpu.get_barrier_semaphore()
    for by in (-2, -1, 1, 2):
        pl.semaphore_signal(
            barrier, inc=1, device_id={"tm": places.time_device(by)}, device_id_type=MESH
        )
    for dx, dy in places.offsets:
        pl.semaphore_signal(
            barrier, inc=1, device_id={"sta": places.station_device(dx, dy)}, device_id_type=MESH
        )


def await_greetings(places):
    pl.semaphore_wait(pltpu.get_barrier_semaphore(), 4 + len(places.offsets))


def start_halo(places, slab, window, halo_send, halo_recv):
    def halo(slot, by, src, dst, width):
        return pltpu.make_async_remote_copy(
            src_ref=window.at[:, pl.ds(src, width)],
            dst_ref=window.at[:, pl.ds(dst, width)],
            send_sem=halo_send.at[slot],
            recv_sem=halo_recv.at[slot],
            device_id={"tm": places.time_device(by)},
            device_id_type=MESH,
        )

    rest = (BLOCKS + 1) * LANE - (LANE + 2 * slab)
    halos = [
        halo(0, -2, LANE, LANE + 2 * slab, rest),
        halo(1, -1, LANE, LANE + slab, slab),
        halo(2, 1, slab, 0, LANE),
    ]
    for copy in halos:
        copy.start()
    return halos


def await_halo(halos):
    for copy in halos:
        copy.wait()


def prepare_template(values):
    values = values.astype(jnp.float32)
    mean = jnp.sum(values, axis=0, keepdims=True) * (1.0 / TLEN)
    centred = values - mean
    power = jnp.sum(centred * centred, axis=0, keepdims=True) * (1.0 / TLEN)
    factor = lax.rsqrt(power + 1e-06) * (1.0 / math.sqrt(TLEN))
    scaled = centred * factor
    return jnp.transpose(scaled).astype(jnp.bfloat16)


def prepare_templates(raw_templates, unit):
    for c in range(unit.shape[0]):
        unit[c] = prepare_template(raw_templates[c])


def bandpass(places, slab, window, bands):
    first = jnp.where(places.me_t == 0, 0.0, window[:, 0:LANE])
    raw = [first] + [window[:, LANE * b : LANE * (b + 1)] for b in range(1, BLOCKS + 1)]
    lows = jnp.concatenate(raw[:BLOCKS], axis=0)
    highs = jnp.concatenate(raw[1:], axis=0)
    filtered = jnp.dot(
        jnp.concatenate([lows, highs], axis=1),
        bands,
        precision=lax.Precision.HIGHEST,
        preferred_element_type=jnp.float32,
    )
    remaining = (places.tm_count - places.me_t) * slab
    return [
        jnp.where(b * LANE < remaining, filtered[8 * b : 8 * b + 8], 0.0) for b in range(BLOCKS)
    ]


def window_norm(blocks, mask):
    series = jnp.concatenate(blocks, axis=1)
    level = jnp.concatenate([series, series * series], axis=0)
    kept = {}
    for bit in range(9):
        if bit in (4, 7, 8):
            kept[bit] = level
        if bit < 8:
            level = level + shifted_left(level, 1 << bit)
    sums = kept[8] + shifted_left(kept[7], 256) + shifted_left(kept[4], 384)
    window_sum, window_power = sums[0:8, : 8 * LANE], sums[8:16, : 8 * LANE]
    inverse_norm = lax.rsqrt(
        jnp.maximum(window_power - window_sum * window_sum * (1.0 / TLEN), 1.0)
    )
    row = lax.broadcasted_iota(jnp.int32, (8, 8 * LANE), 0)
    return inverse_norm * jnp.where(row < 3, mask[0], mask[1]).astype(jnp.float32)


def build_hankel(blocks, hankel):
    lane = lax.broadcasted_iota(jnp.int32, (LANE, LANE), 1)
    line = lax.broadcasted_iota(jnp.int32, (LANE, LANE), 0)
    inside = lane + line < LANE
    turn = lax.rem(lane + line, LANE)
    for c in range(hankel.shape[0]):
        turned = [
            jnp.take_along_axis(
                jnp.broadcast_to(blocks[b][c : c + 1], (LANE, LANE)),
                turn,
                axis=1,
                mode="promise_in_bounds",
            )
            for b in range(BLOCKS)
        ]
        turned.append(jnp.zeros((LANE, LANE), jnp.float32))
        for b in range(BLOCKS):
            hankel[c, :, LANE * b : LANE * (b + 1)] = jnp.where(
                inside, turned[b], turned[b + 1]
            ).astype(jnp.bfloat16)


def correlate(c, rows, unit, hankel):
    matrix = jnp.concatenate(
        [
            hankel[c, 0 : min(LANE, TLEN - LANE * m), LANE * m : LANE * (m + 8)]
            for m in range(4)
        ],
        axis=0,
    )
    return jnp.dot(rows, matrix, preferred_element_type=jnp.float32)


def moved(products, inverse_norm, delay):
    rows = products.shape[0]
    lane = lax.broadcasted_iota(jnp.int32, (rows, LANE), 1)
    by_256 = delay >= 256
    by_128 = lax.rem(delay, 256) >= 128
    fine = lax.rem(delay, 128)
    p = [
        products[:, LANE * b : LANE * (b + 1)] * inverse_norm[:, LANE * b : LANE * (b + 1)]
        for b in range(8)
    ]
    p = [jnp.where(by_256, p[b + 2], p[b]) for b in range(6)]
    p = [jnp.where(by_128, p[b + 1], p[b]) for b in range(5)]
    source = lax.rem(lane + fine, LANE)
    ahead = lane < fine
    return [
        jnp.take_along_axis(
            jnp.where(ahead, p[b + 1], p[b]), source, axis=1, mode="promise_in_bounds"
        )
        for b in range(4)
    ]


def match(peers, share, delays, inverse_norm, unit, hankel, partial):
    count = len(peers) * share
    starts = [pl.multiple_of(peer * share, share) for peer in peers]
    total = None
    for c in range(unit.shape[0]):
        rows = jnp.concatenate([unit[c, pl.ds(start, share), :] for start in starts], axis=0)
        products = correlate(c, rows, unit, hankel)
        delay = jnp.concatenate([delays[pl.ds(start, share), c : c + 1] for start in starts], axis=0)
        terms = moved(products, inverse_norm[c : c + 1], jnp.broadcast_to(delay, (count, LANE)))
        total = terms if total is None else [a + b for a, b in zip(total, terms)]
    for i, start in enumerate(starts):
        for b in range(4):
            partial[pl.ds(start, share), LANE * b : LANE * (b + 1)] = total[b][
                share * i : share * (i + 1)
            ]


def send_sum(places, share, slot, peer, partial, received, sum_send, sum_recv):
    copy = pltpu.make_async_remote_copy(
        src_ref=partial.at[pl.ds(pl.multiple_of(peer * share, share), share)],
        dst_ref=received.at[slot],
        send_sem=sum_send.at[slot],
        recv_sem=sum_recv.at[slot],
        device_id={"sta": peer},
        device_id_type=MESH,
    )
    copy.start()
    return copy


def add_received(places, share, copies, partial, received, out_ref):
    result = partial[pl.ds(pl.multiple_of(places.me_s * share, share), share), :]
    for slot, copy in copies:
        copy.wait()
        result = result + received[slot]
    out_ref[...] = result


def chunks_of(places):
    far = sorted(places.offsets, key=lambda o: -(min(o[0], places.x_count - o[0]) + 2 * o[1]))
    far.append((0, 0))
    groups = [far[sum(CHUNKS[:i]) : sum(CHUNKS[: i + 1])] for i in range(len(CHUNKS))]
    return [group for group in groups if group]


def kernel(
    sizes,
    traces_ref,
    taps_ref,
    templates_ref,
    moveouts_ref,
    mask_ref,
    out_ref,
    samples,
    taps,
    moveouts,
    mask,
    window,
    raw_templates,
    unit,
    delays,
    hankel,
    partial,
    received,
    local_sem,
    halo_send,
    halo_recv,
    sum_send,
    sum_recv,
):
    slab, channels, share = sizes[2:]
    kcount = share * sizes[1]
    places = Places(sizes)
    fetches = [
        pltpu.make_async_copy(src, dst, local_sem.at[i])
        for i, (src, dst) in enumerate(
            [(traces_ref, samples), (taps_ref, taps), (moveouts_ref, moveouts), (mask_ref, mask)]
            + [(templates_ref.at[c], raw_templates.at[c]) for c in range(channels)]
        )
    ]
    for fetch in fetches:
        fetch.start()
    greet(places)
    fetches[0].wait()
    window[0:channels, LANE : LANE + slab] = samples[...]
    window[channels:8, LANE : LANE + slab] = jnp.zeros((8 - channels, slab), jnp.float32)
    await_greetings(places)
    halos = start_halo(places, slab, window, halo_send, halo_recv)
    fetches[1].wait()
    bands = toeplitz(taps[...])
    fetches[2].wait()
    delays[:, 0:8] = jnp.transpose(
        jnp.concatenate([moveouts[...], jnp.zeros((8 - channels, kcount), jnp.int32)], axis=0)
    )
    for fetch in fetches[3:]:
        fetch.wait()
    prepare_templates(raw_templates, unit)
    await_halo(halos)
    blocks = bandpass(places, slab, window, bands)
    inverse_norm = window_norm(blocks, mask)
    build_hankel(blocks, hankel)
    copies = []
    for chunk in chunks_of(places):
        peers = [places.station_device(dx, dy) for dx, dy in chunk]
        match(peers, share, delays, inverse_norm, unit, hankel, partial)
        for offset, peer in zip(chunk, peers):
            if offset != (0, 0):
                slot = places.offsets.index(offset)
                copy = send_sum(places, share, slot, peer, partial, received, sum_send, sum_recv)
                copies.append((slot, copy))
    add_received(places, share, copies, partial, received, out_ref)


def per_device(sizes, traces, taps, templates, moveouts, mask):
    tm_count, sta_count, slab, channels, share = sizes
    kcount = share * sta_count
    vmem = pl.BlockSpec(memory_space=pltpu.VMEM)
    hbm = pl.BlockSpec(memory_space=pltpu.HBM)
    return pl.pallas_call(
        functools.partial(kernel, sizes),
        out_shape=jax.ShapeDtypeStruct((share, slab), jnp.float32),
        in_specs=[hbm] * 5,
        out_specs=vmem,
        scratch_shapes=[
            pltpu.VMEM((channels, slab), jnp.float32),
            pltpu.VMEM((1, LANE), jnp.float32),
            pltpu.VMEM((channels, kcount), jnp.int32),
            pltpu.SMEM((2,), jnp.int32),
            pltpu.VMEM((8, (BLOCKS + 1) * LANE), jnp.float32),
            pltpu.VMEM((channels, TLEN, kcount), jnp.bfloat16),
            pltpu.VMEM((channels, kcount, TLEN), jnp.bfloat16),
            pltpu.VMEM((kcount, LANE), jnp.int32),
            pltpu.VMEM((channels, LANE, BLOCKS * LANE), jnp.bfloat16),
            pltpu.VMEM((kcount, slab), jnp.float32),
            pltpu.VMEM((sta_count - 1, share, slab), jnp.float32),
            pltpu.SemaphoreType.DMA((4 + channels,)),
            pltpu.SemaphoreType.DMA((3,)),
            pltpu.SemaphoreType.DMA((3,)),
            pltpu.SemaphoreType.DMA((sta_count - 1,)),
            pltpu.SemaphoreType.DMA((sta_count - 1,)),
        ],
        compiler_params=pltpu.CompilerParams(
            collective_id=0, has_side_effects=True, vmem_limit_bytes=24 * 2**20
        ),
        cost_estimate=pl.CostEstimate(
            flops=2 * kcount * channels * 512 * 1024, bytes_accessed=4 * 2**20, transcendentals=0
        ),
        name="network_match",
    )(
        *(
            pltpu.with_memory_space_constraint(array, pltpu.HBM)
            for array in (
                traces,
                taps.reshape(1, LANE),
                jnp.transpose(templates, (1, 2, 0)),
                jnp.transpose(moveouts),
                mask,
            )
        )
    )


def solution(mesh):
    tm_count, sta_count = mesh.shape["tm"], mesh.shape["sta"]

    def run(traces, taps, templates, moveouts, mask):
        sizes = (
            tm_count,
            sta_count,
            traces.shape[1] // tm_count,
            traces.shape[0] // sta_count,
            templates.shape[0] // sta_count,
        )
        return jax.shard_map(
            functools.partial(per_device, sizes),
            mesh=mesh,
            in_specs=(P("sta", "tm"), P(), P(None, "sta", None), P(None, "sta"), P("sta")),
            out_specs=P("sta", "tm"),
            check_vma=False,
        )(traces, taps, templates, moveouts, mask)

    return run
```

time: 33.9 us -> 27.2 us (0.80)
  the two profiles are of different devices: /device:TPU:4 before, /device:TPU:2 now
where the time goes in v2:
time: 27.2 us; the launch traced here: 27 us
  Pallas kernels  26.4 us (97%)
  local copies, waits for them, and re-layouts  0.63 us (2%)
    pallas_call x1, Pallas kernels, per_device(): pl.pallas_call(functools.partial(kernel, sizes), out_shape=jax.ShapeDtype...  26.4 us
    unnamed x1, local copies, waits for them, and re-layouts  0.63 us

profile of v2, /device:TPU:2, one launch (start us, length us, event | category | flops | bytes accessed | tf_op | source)
XLA Modules:
  0.0 27.0 jit_solution(17642791828728261907)
XLA Ops:
  0.0 26.4 %network_match.1 = f32[32,512]{1,0:T(8,128)S(1)} custom-call(f32[6,512]{1,0:T(8,128)} %traces_ref.1, f32[1,128]{1,0:T(1,128)} %bitcast.5, bf16[6,400,256]{2,1,0:T(8,128)(2,1)} %bitcast.3, s32[6,256]{1,0:T(8,128)} %bitcast.4, s32[2]{0:T(128)} %mask_ref.1), custom_call_target="tpu_custom_call" | custom-call | flops 1610612736 | bytes 4194304 | tf_op jit(solution)/shard_map/network_match/pallas_call | solution.py:323
  26.4 0.6 %copy.7 = f32[32,512]{1,0:T(8,128)} copy(f32[32,512]{1,0:T(8,128)S(1)} %network_match.1) | data formatting | bytes 131072

commit v3 on v2

--- a/solution.py
+++ b/solution.py
@@ -45,9 +45,15 @@
         self.offsets = [
             (dx, dy) for dx in range(self.x_count) for dy in range(2) if (dx, dy) != (0, 0)
         ]
+        self.order = sorted(
+            self.offsets, key=lambda o: -(min(o[0], self.x_count - o[0]) + 2 * o[1])
+        ) + [(0, 0)]
 
     def time_device(self, by):
-        return lax.rem(self.me_t + by + self.tm_count, self.tm_count)
+        return self.me_t + by
+
+    def has(self, by):
+        return self.me_t + by >= 0 if by < 0 else self.me_t + by < self.tm_count
 
     def station_device(self, dx, dy):
         x = lax.rem(self.me_s // 2 + dx, self.x_count)
@@ -57,9 +63,13 @@
 def greet(places):
     barrier = pltpu.get_barrier_semaphore()
     for by in (-2, -1, 1, 2):
-        pl.semaphore_signal(
-            barrier, inc=1, device_id={"tm": places.time_device(by)}, device_id_type=MESH
-        )
+
+        @pl.when(places.has(by))
+        def _():
+            pl.semaphore_signal(
+                barrier, inc=1, device_id={"tm": places.time_device(by)}, device_id_type=MESH
+            )
+
     for dx, dy in places.offsets:
         pl.semaphore_signal(
             barrier, inc=1, device_id={"sta": places.station_device(dx, dy)}, device_id_type=MESH
@@ -67,12 +77,13 @@
 
 
 def await_greetings(places):
-    pl.semaphore_wait(pltpu.get_barrier_semaphore(), 4 + len(places.offsets))
-
-
-def start_halo(places, slab, window, halo_send, halo_recv):
+    near = sum(jnp.where(places.has(by), 1, 0) for by in (-2, -1, 1, 2))
+    pl.semaphore_wait(pltpu.get_barrier_semaphore(), near + len(places.offsets))
+
+
+def halo_copies(places, slab, window, halo_send, halo_recv):
     def halo(slot, by, src, dst, width):
-        return pltpu.make_async_remote_copy(
+        copy = pltpu.make_async_remote_copy(
             src_ref=window.at[:, pl.ds(src, width)],
             dst_ref=window.at[:, pl.ds(dst, width)],
             send_sem=halo_send.at[slot],
@@ -80,21 +91,26 @@
             device_id={"tm": places.time_device(by)},
             device_id_type=MESH,
         )
+        return copy, by
 
     rest = (BLOCKS + 1) * LANE - (LANE + 2 * slab)
-    halos = [
+    return [
         halo(0, -2, LANE, LANE + 2 * slab, rest),
         halo(1, -1, LANE, LANE + slab, slab),
         halo(2, 1, slab, 0, LANE),
     ]
-    for copy in halos:
-        copy.start()
-    return halos
-
-
-def await_halo(halos):
-    for copy in halos:
-        copy.wait()
+
+
+def start_halo(places, halos):
+    for copy, by in halos:
+        pl.when(places.has(by))(copy.start)
+
+
+def await_halo(places, halos):
+    for copy, by in halos:
+        pl.when(places.has(-by))(copy.wait_recv)
+    for copy, by in halos:
+        pl.when(places.has(by))(copy.wait_send)
 
 
 def prepare_template(values):
@@ -107,9 +123,17 @@
     return jnp.transpose(scaled).astype(jnp.bfloat16)
 
 
-def prepare_templates(raw_templates, unit):
+def store_in_order(places, share, rows, ref):
+    order = [places.station_device(dx, dy) for dx, dy in places.order]
+    for block in range(places.sta_count):
+        slot = sum(jnp.where(peer == block, i, 0) for i, peer in enumerate(order))
+        start = pl.multiple_of(slot * share, share)
+        ref[pl.ds(start, share), :] = rows[share * block : share * (block + 1)]
+
+
+def prepare_templates(places, share, raw_templates, unit):
     for c in range(unit.shape[0]):
-        unit[c] = prepare_template(raw_templates[c])
+        store_in_order(places, share, prepare_template(raw_templates[c]), unit.at[c])
 
 
 def bandpass(places, slab, window, bands):
@@ -202,30 +226,24 @@
     ]
 
 
-def match(peers, share, delays, inverse_norm, unit, hankel, partial):
-    count = len(peers) * share
-    starts = [pl.multiple_of(peer * share, share) for peer in peers]
+def match(first, count, delays, inverse_norm, unit, hankel, partial):
     total = None
     for c in range(unit.shape[0]):
-        rows = jnp.concatenate([unit[c, pl.ds(start, share), :] for start in starts], axis=0)
-        products = correlate(c, rows, unit, hankel)
-        delay = jnp.concatenate([delays[pl.ds(start, share), c : c + 1] for start in starts], axis=0)
-        terms = moved(products, inverse_norm[c : c + 1], jnp.broadcast_to(delay, (count, LANE)))
+        products = correlate(c, unit[c, first : first + count, :], unit, hankel)
+        delay = jnp.broadcast_to(delays[first : first + count, c : c + 1], (count, LANE))
+        terms = moved(products, inverse_norm[c : c + 1], delay)
         total = terms if total is None else [a + b for a, b in zip(total, terms)]
-    for i, start in enumerate(starts):
-        for b in range(4):
-            partial[pl.ds(start, share), LANE * b : LANE * (b + 1)] = total[b][
-                share * i : share * (i + 1)
-            ]
-
-
-def send_sum(places, share, slot, peer, partial, received, sum_send, sum_recv):
+    for b in range(4):
+        partial[first : first + count, LANE * b : LANE * (b + 1)] = total[b]
+
+
+def send_sum(places, share, slot, partial, received, sum_send, sum_recv):
     copy = pltpu.make_async_remote_copy(
-        src_ref=partial.at[pl.ds(pl.multiple_of(peer * share, share), share)],
+        src_ref=partial.at[pl.ds(share * slot, share)],
         dst_ref=received.at[slot],
         send_sem=sum_send.at[slot],
         recv_sem=sum_recv.at[slot],
-        device_id={"sta": peer},
+        device_id={"sta": places.station_device(*places.order[slot])},
         device_id_type=MESH,
     )
     copy.start()
@@ -233,18 +251,11 @@
 
 
 def add_received(places, share, copies, partial, received, out_ref):
-    result = partial[pl.ds(pl.multiple_of(places.me_s * share, share), share), :]
-    for slot, copy in copies:
+    result = partial[share * len(copies) :, :]
+    for slot, copy in enumerate(copies):
         copy.wait()
         result = result + received[slot]
     out_ref[...] = result
-
-
-def chunks_of(places):
-    far = sorted(places.offsets, key=lambda o: -(min(o[0], places.x_count - o[0]) + 2 * o[1]))
-    far.append((0, 0))
-    groups = [far[sum(CHUNKS[:i]) : sum(CHUNKS[: i + 1])] for i in range(len(CHUNKS))]
-    return [group for group in groups if group]
 
 
 def kernel(
@@ -284,34 +295,34 @@
     ]
     for fetch in fetches:
         fetch.start()
+    window[...] = jnp.zeros_like(window)
     greet(places)
     fetches[0].wait()
     window[0:channels, LANE : LANE + slab] = samples[...]
-    window[channels:8, LANE : LANE + slab] = jnp.zeros((8 - channels, slab), jnp.float32)
     await_greetings(places)
-    halos = start_halo(places, slab, window, halo_send, halo_recv)
+    halos = halo_copies(places, slab, window, halo_send, halo_recv)
+    start_halo(places, halos)
     fetches[1].wait()
     bands = toeplitz(taps[...])
     fetches[2].wait()
-    delays[:, 0:8] = jnp.transpose(
+    turned = jnp.transpose(
         jnp.concatenate([moveouts[...], jnp.zeros((8 - channels, kcount), jnp.int32)], axis=0)
     )
+    store_in_order(places, share, turned, delays)
     for fetch in fetches[3:]:
         fetch.wait()
-    prepare_templates(raw_templates, unit)
-    await_halo(halos)
+    prepare_templates(places, share, raw_templates, unit)
+    await_halo(places, halos)
     blocks = bandpass(places, slab, window, bands)
     inverse_norm = window_norm(blocks, mask)
     build_hankel(blocks, hankel)
     copies = []
-    for chunk in chunks_of(places):
-        peers = [places.station_device(dx, dy) for dx, dy in chunk]
-        match(peers, share, delays, inverse_norm, unit, hankel, partial)
-        for offset, peer in zip(chunk, peers):
-            if offset != (0, 0):
-                slot = places.offsets.index(offset)
-                copy = send_sum(places, share, slot, peer, partial, received, sum_send, sum_recv)
-                copies.append((slot, copy))
+    first = 0
+    for group in CHUNKS:
+        match(first * share, group * share, delays, inverse_norm, unit, hankel, partial)
+        for slot in range(first, min(first + group, places.sta_count - 1)):
+            copies.append(send_sum(places, share, slot, partial, received, sum_send, sum_recv))
+        first += group
     add_received(places, share, copies, partial, received, out_ref)
 
 
@@ -333,7 +344,7 @@
             pltpu.VMEM((8, (BLOCKS + 1) * LANE), jnp.float32),
             pltpu.VMEM((channels, TLEN, kcount), jnp.bfloat16),
             pltpu.VMEM((channels, kcount, TLEN), jnp.bfloat16),
-            pltpu.VMEM((kcount, LANE), jnp.int32),
+            pltpu.VMEM((kcount, 8), jnp.int32),
             pltpu.VMEM((channels, LANE, BLOCKS * LANE), jnp.bfloat16),
             pltpu.VMEM((kcount, slab), jnp.float32),
             pltpu.VMEM((sta_count - 1, share, slab), jnp.float32),

time: 27.2 us -> 24 us (0.88)
  the two profiles are of different devices: /device:TPU:2 before, /device:TPU:232 now
where the time goes in v3:
time: 24 us; the launch traced here: 23.7 us
  Pallas kernels  23.1 us (96%)
  local copies, waits for them, and re-layouts  0.63 us (3%)
    pallas_call x1, Pallas kernels, per_device(): pl.pallas_call(functools.partial(kernel, sizes), out_shape=jax.ShapeDtype...  23.1 us
    unnamed x1, local copies, waits for them, and re-layouts  0.63 us

profile of v3, /device:TPU:232, one launch (start us, length us, event | category | flops | bytes accessed | tf_op | source)
XLA Modules:
  0.0 23.7 jit_solution(9262862234909995320)
XLA Ops:
  0.0 23.1 %network_match.1 = f32[32,512]{1,0:T(8,128)S(1)} custom-call(f32[6,512]{1,0:T(8,128)} %traces_ref.1, f32[1,128]{1,0:T(1,128)} %bitcast.5, bf16[6,400,256]{2,1,0:T(8,128)(2,1)} %bitcast.3, s32[6,256]{1,0:T(8,128)} %bitcast.4, s32[2]{0:T(128)} %mask_ref.1), custom_call_target="tpu_custom_call" | custom-call | flops 1610612736 | bytes 4194304 | tf_op jit(solution)/shard_map/network_match/pallas_call | solution.py:334
  23.1 0.6 %copy.7 = f32[32,512]{1,0:T(8,128)} copy(f32[32,512]{1,0:T(8,128)S(1)} %network_match.1) | data formatting | bytes 131072

commit v4 on v3

--- a/solution.py
+++ b/solution.py
@@ -109,6 +109,9 @@
 def await_halo(places, halos):
     for copy, by in halos:
         pl.when(places.has(-by))(copy.wait_recv)
+
+
+def finish_halo(places, halos):
     for copy, by in halos:
         pl.when(places.has(by))(copy.wait_send)
 
@@ -120,7 +123,10 @@
     power = jnp.sum(centred * centred, axis=0, keepdims=True) * (1.0 / TLEN)
     factor = lax.rsqrt(power + 1e-06) * (1.0 / math.sqrt(TLEN))
     scaled = centred * factor
-    return jnp.transpose(scaled).astype(jnp.bfloat16)
+    groups = scaled.reshape(TLEN // 8, 8, values.shape[1])
+    back = 7 - lax.broadcasted_iota(jnp.int32, groups.shape, 1)
+    reversed_groups = jnp.take_along_axis(groups, back, axis=1, mode="promise_in_bounds")
+    return jnp.transpose(reversed_groups.reshape(scaled.shape)).astype(jnp.bfloat16)
 
 
 def store_in_order(places, share, rows, ref):
@@ -153,17 +159,27 @@
     ]
 
 
+def window_bands():
+    row = lax.broadcasted_iota(jnp.int32, (5 * LANE, LANE), 0)
+    lane = lax.broadcasted_iota(jnp.int32, (5 * LANE, LANE), 1)
+    ahead = row - lane
+    return jnp.where((ahead >= 0) & (ahead < TLEN), 1.0, 0.0).astype(jnp.bfloat16)
+
+
 def window_norm(blocks, mask):
-    series = jnp.concatenate(blocks, axis=1)
-    level = jnp.concatenate([series, series * series], axis=0)
-    kept = {}
-    for bit in range(9):
-        if bit in (4, 7, 8):
-            kept[bit] = level
-        if bit < 8:
-            level = level + shifted_left(level, 1 << bit)
-    sums = kept[8] + shifted_left(kept[7], 256) + shifted_left(kept[4], 384)
-    window_sum, window_power = sums[0:8, : 8 * LANE], sums[8:16, : 8 * LANE]
+    padded = blocks + [jnp.zeros((8, LANE), jnp.float32)]
+    both = [jnp.concatenate([block, block * block], axis=0) for block in padded]
+    pieces = []
+    for _ in range(3):
+        rounded = [block.astype(jnp.bfloat16) for block in both]
+        both = [block - part.astype(jnp.float32) for block, part in zip(both, rounded)]
+        pieces += [jnp.concatenate(rounded[b : b + 5], axis=1) for b in range(8)]
+    sums = jnp.dot(
+        jnp.concatenate(pieces, axis=0), window_bands(), preferred_element_type=jnp.float32
+    )
+    sums = (sums[256:384] + sums[128:256]) + sums[0:128]
+    window_sum = jnp.concatenate([sums[16 * b : 16 * b + 8] for b in range(8)], axis=1)
+    window_power = jnp.concatenate([sums[16 * b + 8 : 16 * b + 16] for b in range(8)], axis=1)
     inverse_norm = lax.rsqrt(
         jnp.maximum(window_power - window_sum * window_sum * (1.0 / TLEN), 1.0)
     )
@@ -172,25 +188,23 @@
 
 
 def build_hankel(blocks, hankel):
-    lane = lax.broadcasted_iota(jnp.int32, (LANE, LANE), 1)
-    line = lax.broadcasted_iota(jnp.int32, (LANE, LANE), 0)
-    inside = lane + line < LANE
-    turn = lax.rem(lane + line, LANE)
+    lane = lax.broadcasted_iota(jnp.int32, (8, LANE), 1)
+    line = lax.broadcasted_iota(jnp.int32, (8, LANE), 0)
     for c in range(hankel.shape[0]):
-        turned = [
-            jnp.take_along_axis(
-                jnp.broadcast_to(blocks[b][c : c + 1], (LANE, LANE)),
-                turn,
-                axis=1,
-                mode="promise_in_bounds",
-            )
-            for b in range(BLOCKS)
-        ]
-        turned.append(jnp.zeros((LANE, LANE), jnp.float32))
-        for b in range(BLOCKS):
-            hankel[c, :, LANE * b : LANE * (b + 1)] = jnp.where(
-                inside, turned[b], turned[b + 1]
-            ).astype(jnp.bfloat16)
+        rows = [jnp.broadcast_to(blocks[b][c : c + 1], (8, LANE)) for b in range(BLOCKS)]
+        for g in range(0, 16, 2):
+            halves = []
+            for h in (g, g + 1):
+                turned = [pltpu.roll(row, 121 - 8 * h, 1, stride=1, stride_axis=0) for row in rows]
+                turned.append(jnp.zeros((8, LANE), jnp.float32))
+                inside = lane + (8 * h + 7) - line < LANE
+                halves.append(
+                    [jnp.where(inside, turned[b], turned[b + 1]) for b in range(BLOCKS)]
+                )
+            for b in range(BLOCKS):
+                hankel[c, 8 * g : 8 * g + 16, LANE * b : LANE * (b + 1)] = jnp.concatenate(
+                    [halves[0][b], halves[1][b]], axis=0
+                ).astype(jnp.bfloat16)
 
 
 def correlate(c, rows, unit, hankel):
@@ -253,9 +267,11 @@
 def add_received(places, share, copies, partial, received, out_ref):
     result = partial[share * len(copies) :, :]
     for slot, copy in enumerate(copies):
-        copy.wait()
+        copy.wait_recv()
         result = result + received[slot]
     out_ref[...] = result
+    for copy in copies:
+        copy.wait_send()
 
 
 def kernel(
@@ -324,6 +340,7 @@
             copies.append(send_sum(places, share, slot, partial, received, sum_send, sum_recv))
         first += group
     add_received(places, share, copies, partial, received, out_ref)
+    finish_halo(places, halos)
 
 
 def per_device(sizes, traces, taps, templates, moveouts, mask):

time: 24 us -> 22.3 us (0.929)
  the two profiles are of different devices: /device:TPU:232 before, /device:TPU:105 now
where the time goes in v4:
time: 22.3 us; the launch traced here: 22.1 us
  Pallas kernels  21.5 us (96%)
  local copies, waits for them, and re-layouts  0.63 us (3%)
    pallas_call x1, Pallas kernels, per_device(): pl.pallas_call(functools.partial(kernel, sizes), out_shape=jax.ShapeDtype...  21.5 us
    unnamed x1, local copies, waits for them, and re-layouts  0.63 us

profile of v4, /device:TPU:105, one launch (start us, length us, event | category | flops | bytes accessed | tf_op | source)
XLA Modules:
  0.0 22.1 jit_solution(4395313896465803845)
XLA Ops:
  0.0 21.5 %network_match.1 = f32[32,512]{1,0:T(8,128)S(1)} custom-call(f32[6,512]{1,0:T(8,128)} %traces_ref.1, f32[1,128]{1,0:T(1,128)} %bitcast.5, bf16[6,400,256]{2,1,0:T(8,128)(2,1)} %bitcast.3, s32[6,256]{1,0:T(8,128)} %bitcast.4, s32[2]{0:T(128)} %mask_ref.1), custom_call_target="tpu_custom_call" | custom-call | flops 1610612736 | bytes 4194304 | tf_op jit(solution)/shard_map/network_match/pallas_call | solution.py:351
  21.5 0.6 %copy.7 = f32[32,512]{1,0:T(8,128)} copy(f32[32,512]{1,0:T(8,128)S(1)} %network_match.1) | data formatting | bytes 131072

commit v5 on v4

--- a/solution.py
+++ b/solution.py
@@ -45,6 +45,19 @@
         self.offsets = [
             (dx, dy) for dx in range(self.x_count) for dy in range(2) if (dx, dy) != (0, 0)
         ]
+        x, y = lax.shift_right_logical(self.me_s, 1), self.me_s & 1
+        at_start = self.me_t == 0
+
+        def turn(x, y):
+            first = at_start & (x + y == 0)
+            return jnp.where(first, self.sta_count, y * self.x_count + x)
+
+        mine = turn(x, y)
+        self.peers, self.later = {(0, 0): self.me_s}, {}
+        for dx, dy in self.offsets:
+            peer_x, peer_y = (x + dx) & (self.x_count - 1), y ^ dy
+            self.peers[dx, dy] = 2 * peer_x + peer_y
+            self.later[dx, dy] = turn(peer_x, peer_y) < mine
         self.order = sorted(
             self.offsets, key=lambda o: -(min(o[0], self.x_count - o[0]) + 2 * o[1])
         ) + [(0, 0)]
@@ -55,30 +68,77 @@
     def has(self, by):
         return self.me_t + by >= 0 if by < 0 else self.me_t + by < self.tm_count
 
+    def last_to_come(self, by):
+        if by > 0:
+            return self.me_t == 0
+        return self.me_t + by != 0
+
+    def later_peer(self, dx, dy):
+        return self.later[dx, dy]
+
     def station_device(self, dx, dy):
-        x = lax.rem(self.me_s // 2 + dx, self.x_count)
-        return 2 * x + lax.rem(lax.rem(self.me_s, 2) + dy, 2)
+        return self.peers[dx, dy]
 
 
 def greet(places):
     barrier = pltpu.get_barrier_semaphore()
     for by in (-2, -1, 1, 2):
 
-        @pl.when(places.has(by))
+        @pl.when(places.has(by) & jnp.logical_not(places.last_to_come(by)))
         def _():
             pl.semaphore_signal(
                 barrier, inc=1, device_id={"tm": places.time_device(by)}, device_id_type=MESH
             )
 
     for dx, dy in places.offsets:
-        pl.semaphore_signal(
-            barrier, inc=1, device_id={"sta": places.station_device(dx, dy)}, device_id_type=MESH
-        )
+
+        @pl.when(jnp.logical_not(places.later_peer(dx, dy)))
+        def _():
+            pl.semaphore_signal(
+                barrier,
+                inc=1,
+                device_id={"sta": places.station_device(dx, dy)},
+                device_id_type=MESH,
+            )
 
 
 def await_greetings(places):
-    near = sum(jnp.where(places.has(by), 1, 0) for by in (-2, -1, 1, 2))
-    pl.semaphore_wait(pltpu.get_barrier_semaphore(), near + len(places.offsets))
+    near = sum(
+        jnp.where(places.has(by) & places.last_to_come(by), 1, 0) for by in (-2, -1, 1, 2)
+    )
+    far = sum(jnp.where(places.later_peer(dx, dy), 1, 0) for dx, dy in places.offsets)
+    barrier = pltpu.get_barrier_semaphore()
+
+    @pl.when(near + far > 0)
+    def _():
+        pl.semaphore_wait(barrier, near + far)
+
+
+def answer_near(places, near_sem):
+    for by in (-1, 1, 2):
+
+        @pl.when(places.has(by) & places.last_to_come(by))
+        def _():
+            pl.semaphore_signal(
+                near_sem.at[2 - by],
+                inc=1,
+                device_id={"tm": places.time_device(by)},
+                device_id_type=MESH,
+            )
+
+
+def answer_far(places, far_sem):
+    for dx, dy in places.offsets:
+        back = (-dx % places.x_count, dy)
+
+        @pl.when(places.later_peer(dx, dy))
+        def _():
+            pl.semaphore_signal(
+                far_sem.at[places.offsets.index(back)],
+                inc=1,
+                device_id={"sta": places.station_device(dx, dy)},
+                device_id_type=MESH,
+            )
 
 
 def halo_copies(places, slab, window, halo_send, halo_recv):
@@ -101,9 +161,16 @@
     ]
 
 
-def start_halo(places, halos):
+def start_halo(places, halos, near_sem):
     for copy, by in halos:
-        pl.when(places.has(by))(copy.start)
+        pl.when(places.has(by) & places.last_to_come(by))(copy.start)
+    answer_near(places, near_sem)
+    for copy, by in halos:
+
+        @pl.when(places.has(by) & jnp.logical_not(places.last_to_come(by)))
+        def _():
+            pl.semaphore_wait(near_sem.at[2 + by], 1)
+            copy.start()
 
 
 def await_halo(places, halos):
@@ -251,13 +318,19 @@
         partial[first : first + count, LANE * b : LANE * (b + 1)] = total[b]
 
 
-def send_sum(places, share, slot, partial, received, sum_send, sum_recv):
+def send_sum(places, share, slot, partial, received, far_sem, sum_send, sum_recv):
+    offset = places.order[slot]
+
+    @pl.when(jnp.logical_not(places.later_peer(*offset)))
+    def _():
+        pl.semaphore_wait(far_sem.at[places.offsets.index(offset)], 1)
+
     copy = pltpu.make_async_remote_copy(
         src_ref=partial.at[pl.ds(share * slot, share)],
         dst_ref=received.at[slot],
         send_sem=sum_send.at[slot],
         recv_sem=sum_recv.at[slot],
-        device_id={"sta": places.station_device(*places.order[slot])},
+        device_id={"sta": places.station_device(*offset)},
         device_id_type=MESH,
     )
     copy.start()
@@ -293,6 +366,8 @@
     hankel,
     partial,
     received,
+    near_sem,
+    far_sem,
     local_sem,
     halo_send,
     halo_recv,
@@ -317,7 +392,8 @@
     window[0:channels, LANE : LANE + slab] = samples[...]
     await_greetings(places)
     halos = halo_copies(places, slab, window, halo_send, halo_recv)
-    start_halo(places, halos)
+    start_halo(places, halos, near_sem)
+    answer_far(places, far_sem)
     fetches[1].wait()
     bands = toeplitz(taps[...])
     fetches[2].wait()
@@ -337,7 +413,9 @@
     for group in CHUNKS:
         match(first * share, group * share, delays, inverse_norm, unit, hankel, partial)
         for slot in range(first, min(first + group, places.sta_count - 1)):
-            copies.append(send_sum(places, share, slot, partial, received, sum_send, sum_recv))
+            copies.append(
+                send_sum(places, share, slot, partial, received, far_sem, sum_send, sum_recv)
+            )
         first += group
     add_received(places, share, copies, partial, received, out_ref)
     finish_halo(places, halos)
@@ -365,6 +443,8 @@
             pltpu.VMEM((channels, LANE, BLOCKS * LANE), jnp.bfloat16),
             pltpu.VMEM((kcount, slab), jnp.float32),
             pltpu.VMEM((sta_count - 1, share, slab), jnp.float32),
+            pltpu.SemaphoreType.REGULAR((5,)),
+            pltpu.SemaphoreType.REGULAR((sta_count - 1,)),
             pltpu.SemaphoreType.DMA((4 + channels,)),
             pltpu.SemaphoreType.DMA((3,)),
             pltpu.SemaphoreType.DMA((3,)),

time: 22.3 us -> 20.8 us (0.933)
  the two profiles are of different devices: /device:TPU:105 before, /device:TPU:232 now
where the time goes in v5:
time: 20.8 us; the launch traced here: 20.7 us
  Pallas kernels  20 us (96%)
  local copies, waits for them, and re-layouts  0.63 us (3%)
    pallas_call x1, Pallas kernels, per_device(): pl.pallas_call(functools.partial(kernel, sizes), out_shape=jax.ShapeDtype...  20 us
    unnamed x1, local copies, waits for them, and re-layouts  0.63 us

profile of v5, /device:TPU:232, one launch (start us, length us, event | category | flops | bytes accessed | tf_op | source)
XLA Modules:
  0.0 20.7 jit_solution(1672707046109298486)
XLA Ops:
  0.0 20.0 %network_match.1 = f32[32,512]{1,0:T(8,128)S(1)} custom-call(f32[6,512]{1,0:T(8,128)} %traces_ref.1, f32[1,128]{1,0:T(1,128)} %bitcast.5, bf16[6,400,256]{2,1,0:T(8,128)(2,1)} %bitcast.3, s32[6,256]{1,0:T(8,128)} %bitcast.4, s32[2]{0:T(128)} %mask_ref.1), custom_call_target="tpu_custom_call" | custom-call | flops 1610612736 | bytes 4194304 | tf_op jit(solution)/shard_map/network_match/pallas_call | solution.py:429
  20.0 0.6 %copy.7 = f32[32,512]{1,0:T(8,128)} copy(f32[32,512]{1,0:T(8,128)S(1)} %network_match.1) | data formatting | bytes 131072

commit v6 on v5

--- a/solution.py
+++ b/solution.py
@@ -58,9 +58,7 @@
             peer_x, peer_y = (x + dx) & (self.x_count - 1), y ^ dy
             self.peers[dx, dy] = 2 * peer_x + peer_y
             self.later[dx, dy] = turn(peer_x, peer_y) < mine
-        self.order = sorted(
-            self.offsets, key=lambda o: -(min(o[0], self.x_count - o[0]) + 2 * o[1])
-        ) + [(0, 0)]
+        self.order = [(0,1),(2,1),(1,1),(3,1),(2,0),(1,0),(3,0),(0,0)]
 
     def time_device(self, by):
         return self.me_t + by
@@ -164,7 +162,6 @@
 def start_halo(places, halos, near_sem):
     for copy, by in halos:
         pl.when(places.has(by) & places.last_to_come(by))(copy.start)
-    answer_near(places, near_sem)
     for copy, by in halos:
 
         @pl.when(places.has(by) & jnp.logical_not(places.last_to_come(by)))
@@ -388,9 +385,10 @@
         fetch.start()
     window[...] = jnp.zeros_like(window)
     greet(places)
+    await_greetings(places)
+    answer_near(places, near_sem)
     fetches[0].wait()
     window[0:channels, LANE : LANE + slab] = samples[...]
-    await_greetings(places)
     halos = halo_copies(places, slab, window, halo_send, halo_recv)
     start_halo(places, halos, near_sem)
     answer_far(places, far_sem)

time: 20.8 us -> 20.8 us (level)
  no operation moved by 1% of the time
where the time goes in v6:
time: 20.8 us; the launch traced here: 20.6 us
  Pallas kernels  20 us (96%)
  local copies, waits for them, and re-layouts  0.63 us (3%)
    pallas_call x1, Pallas kernels, per_device(): pl.pallas_call(functools.partial(kernel, sizes), out_shape=jax.ShapeDtype...  20 us
    unnamed x1, local copies, waits for them, and re-layouts  0.63 us

profile of v6, /device:TPU:232, one launch (start us, length us, event | category | flops | bytes accessed | tf_op | source)
XLA Modules:
  0.0 20.6 jit_solution(6249817540502296610)
XLA Ops:
  0.0 20.0 %network_match.1 = f32[32,512]{1,0:T(8,128)S(1)} custom-call(f32[6,512]{1,0:T(8,128)} %traces_ref.1, f32[1,128]{1,0:T(1,128)} %bitcast.5, bf16[6,400,256]{2,1,0:T(8,128)(2,1)} %bitcast.3, s32[6,256]{1,0:T(8,128)} %bitcast.4, s32[2]{0:T(128)} %mask_ref.1), custom_call_target="tpu_custom_call" | custom-call | flops 1610612736 | bytes 4194304 | tf_op jit(solution)/shard_map/network_match/pallas_call | solution.py:427
  20.0 0.6 %copy.7 = f32[32,512]{1,0:T(8,128)} copy(f32[32,512]{1,0:T(8,128)S(1)} %network_match.1) | data formatting | bytes 131072

commit v7 on v6

--- a/solution.py
+++ b/solution.py
@@ -336,8 +336,9 @@
 
 def add_received(places, share, copies, partial, received, out_ref):
     result = partial[share * len(copies) :, :]
-    for slot, copy in enumerate(copies):
-        copy.wait_recv()
+    arrival = sorted(range(len(copies)), key=lambda i: (places.order[i][1], places.order[i] == (2, 1)))
+    for slot in arrival:
+        copies[slot].wait_recv()
         result = result + received[slot]
     out_ref[...] = result
     for copy in copies:

time: 20.8 us -> 20.8 us (level)
  no operation moved by 1% of the time
where the time goes in v7:
time: 20.8 us; the launch traced here: 20.6 us
  Pallas kernels  20 us (96%)
  local copies, waits for them, and re-layouts  0.63 us (3%)
    pallas_call x1, Pallas kernels, per_device(): pl.pallas_call(functools.partial(kernel, sizes), out_shape=jax.ShapeDtype...  20 us
    unnamed x1, local copies, waits for them, and re-layouts  0.63 us

profile of v7, /device:TPU:232, one launch (start us, length us, event | category | flops | bytes accessed | tf_op | source)
XLA Modules:
  0.0 20.6 jit_solution(331797391375268029)
XLA Ops:
  0.0 20.0 %network_match.1 = f32[32,512]{1,0:T(8,128)S(1)} custom-call(f32[6,512]{1,0:T(8,128)} %traces_ref.1, f32[1,128]{1,0:T(1,128)} %bitcast.5, bf16[6,400,256]{2,1,0:T(8,128)(2,1)} %bitcast.3, s32[6,256]{1,0:T(8,128)} %bitcast.4, s32[2]{0:T(128)} %mask_ref.1), custom_call_target="tpu_custom_call" | custom-call | flops 1610612736 | bytes 4194304 | tf_op jit(solution)/shard_map/network_match/pallas_call | solution.py:428
  20.0 0.6 %copy.7 = f32[32,512]{1,0:T(8,128)} copy(f32[32,512]{1,0:T(8,128)S(1)} %network_match.1) | data formatting | bytes 131072
